TPU v7x, 32 devices: a whole 2x2x4 slice. The times are simulated.
32 devices in a mesh: prompt: 4 (over y, x), resp: 8 (over z, core).
Axes of the slice: x: 2, y: 2, z: 4, core: 2. Of those that a mesh axis runs over, the one named last changes fastest.
Arguments:
- query: bfloat16 [32, 256, 2048], P(('prompt', 'resp')), may hold values from -6 to 6
- resp_keys: bfloat16 [32, 256, 512], P(('prompt', 'resp')), may hold values from -6 to 6
- resp_values: bfloat16 [32, 256, 512], P(('prompt', 'resp')), may hold values from -6 to 6
- prompt_keys: bfloat16 [8, 32, 512], P(None, 'prompt'), may hold values from -6 to 6
- prompt_values: bfloat16 [8, 32, 512], P(None, 'prompt'), may hold values from -6 to 6
- out_grad: bfloat16 [32, 256, 2048], P(('prompt', 'resp')), may hold values from -6 to 6
- group: int32 [32], replicated, may hold values from 0 to 7
- lengths: int32 [32], P(('prompt', 'resp')), may hold values from 1 to 256, 5120 in all
Outputs:
- query_grad: bfloat16 [32, 256, 2048], P(('prompt', 'resp'))
- resp_key_grad: bfloat16 [32, 256, 512], P(('prompt', 'resp'))
- resp_value_grad: bfloat16 [32, 256, 512], P(('prompt', 'resp'))
- prompt_key_grad: float32 [8, 32, 512], P(None, 'prompt')
- prompt_value_grad: float32 [8, 32, 512], P(None, 'prompt')
Inputs may be any that keep to these rules, and one draw needn't show every extreme that they name: `group`: response r stands on device r of prompt+resp, in the mesh's order. `lengths`: a response's live tokens come first; some response fills all 256 slots.
All inputs are finite; a program needn't handle non-finite values. No bound on the sum of `lengths` on one device may be relied on, other than what follows from the above.
Results may differ from a plain program's by a relative error of at most 0.0097.
Values may be sent and summed in bfloat16 or wider, within the bound.
A program may use at most 64 MiB of HBM per device.

v0:
```python
import functools
import math

import jax
import jax.numpy as jnp
from jax import lax
from jax.experimental import pallas as pl
from jax.experimental.pallas import tpu as pltpu
from jax.sharding import PartitionSpec as P

QH = 16
KVH = 4
HD = 128
GROUP = QH // KVH
TILE = 128
PIECES = 4
MESH = pl.DeviceIdType.MESH
MASKED = -1e30
SCALE = 1.0 / math.sqrt(HD)
NT = (((1,), (1,)), ((), ()))
NN = (((1,), (0,)), ((), ()))
TN = (((0,), (0,)), ((), ()))


def dot(a, b, dims):
    return lax.dot_general(a, b, dims, preferred_element_type=jnp.float32)


def kernel(
    n_p, n_r, order,
    group_ref, length_ref, query_hbm, grad_hbm, rkeys_hbm, rvalues_hbm, pkeys_hbm, pvalues_hbm,
    dquery_hbm, dkey_hbm, dvalue_hbm, total_ref,
    query_v, grad_v, live_grad_v, keys_v, values_v, pkeys_v, pvalues_v,
    bias_v, weight_v, dprob_v, stat_v, dfront_v, dquery_v, dkey_v, dvalue_v,
    front_send, front_recv, part_send, part_recv, total_v,
    load_sem, store_sem, front_ssem, front_rsem, part_ssem, part_rsem, total_ssem, total_rsem,
):
    rows = query_v.shape[0]
    prompts, own = pkeys_v.shape[:2]
    front = own * n_p
    tiles = rows // TILE
    wide = GROUP * HD
    n_dev = n_p * n_r
    me_p = lax.axis_index("prompt")
    me_r = lax.axis_index("resp")
    me = me_p * n_r + me_r
    stride = n_r // KVH
    power = SCALE * math.log2(math.e)

    barrier = pltpu.get_barrier_semaphore()

    def ahead(place, step, size):
        later = place + step
        return jnp.where(later >= size, later - size, later)

    peers_p = [ahead(me_p, step, n_p) for step in range(n_p)]
    peers_r = [ahead(me_r, step, n_r) for step in range(n_r)]
    for to_p in peers_p:
        for to_r in peers_r:
            if to_p is not peers_p[0] or to_r is not peers_r[0]:
                pl.semaphore_signal(
                    barrier, inc=1, device_id=(to_p, to_r), device_id_type=MESH)

    loads = {}
    resp = pl.ds(front, rows)
    wanted = [("k", rkeys_hbm.at[0], keys_v.at[resp])]
    for h in order:
        cols = pl.ds(h * wide, wide)
        wanted.append((("q", h), query_hbm.at[0, :, cols], query_v.at[:, cols]))
        wanted.append((("g", h), grad_hbm.at[0, :, cols], grad_v.at[:, cols]))
        if h == order[0]:
            wanted.append(("v", rvalues_hbm.at[0], values_v.at[resp]))
            wanted.append(("pk", pkeys_hbm, pkeys_v))
            wanted.append(("pv", pvalues_hbm, pvalues_v))
    for n, (name, src, dst) in enumerate(wanted):
        loads[name] = pltpu.make_async_copy(src, dst, load_sem.at[n])
        loads[name].start()

    live = jnp.where(
        lax.broadcasted_iota(jnp.int32, (rows, HD), 0) < length_ref[0], 1.0, 0.0
    ).astype(jnp.bfloat16)
    bias_v[...] = jnp.where(
        lax.broadcasted_iota(jnp.int32, (TILE, TILE), 0)
        <= lax.broadcasted_iota(jnp.int32, (TILE, TILE), 1), 0.0, MASKED)

    def stacked(ref, h, t, start=0, stop=GROUP):
        return jnp.concatenate(
            [ref[t * TILE:(t + 1) * TILE, (h * GROUP + g) * HD:(h * GROUP + g + 1) * HD]
             for g in range(start, stop)], 0)

    def lanes_of(h):
        return slice(h * HD, (h + 1) * HD)

    def resp_scores(i):
        h = order[i]
        lanes = lanes_of(h)
        loads["q", h].wait()
        loads["g", h].wait()
        for t in range(tiles):
            depth = (t + 1) * TILE
            for g in range(0, GROUP, 2):
                query = stacked(query_v, h, t, g, g + 2)
                grad = stacked(grad_v, h, t, g, g + 2) * jnp.concatenate(
                    [live[t * TILE:(t + 1) * TILE]] * 2, 0)
                span = slice(g * TILE, (g + 2) * TILE)
                live_grad_v[h, t, span] = grad
                scores = dot(keys_v[front:front + depth, lanes], query, NT)
                last = scores[depth - TILE:] + jnp.concatenate([bias_v[...]] * 2, 1)
                scores = jnp.concatenate([scores[:depth - TILE], last], 0) if t else last
                top = jnp.max(scores, 0, keepdims=True)
                weights = jnp.exp2((scores - top) * power)
                dprob = dot(values_v[front:front + depth, lanes], grad, NT)
                weight_v[h, t, 0:depth, span] = weights
                dprob_v[h, t, 0:depth, span] = dprob
                stat_v[h, t, 0:1, span] = top
                stat_v[h, t, 1:2, span] = jnp.sum(weights, 0, keepdims=True)
                stat_v[h, t, 2:3, span] = jnp.sum(weights * dprob, 0, keepdims=True)

    def part_copy(i, step):
        to = peers_p[step]
        return pltpu.make_async_remote_copy(
            src_ref=part_send.at[i, to], dst_ref=part_recv.at[me],
            send_sem=part_ssem.at[i, step], recv_sem=part_rsem,
            device_id=(to, order[i] * stride), device_id_type=MESH)

    def front_terms(i):
        h = order[i]
        lanes = lanes_of(h)
        front_key, front_value = 0.0, 0.0
        for t in range(tiles):
            query = stacked(query_v, h, t)
            grad = live_grad_v[h, t]
            resp_top = stat_v[h, t, 0:1]
            scores = dot(keys_v[0:front, lanes], query, NT)
            dprob = dot(values_v[0:front, lanes], grad, NT)
            top = jnp.maximum(resp_top, jnp.max(scores, 0, keepdims=True))
            shrink = jnp.exp2((resp_top - top) * power)
            weights = jnp.exp2((scores - top) * power)
            inverse = 1.0 / (shrink * stat_v[h, t, 1:2] + jnp.sum(weights, 0, keepdims=True))
            factor = shrink * inverse
            prob = weights * inverse
            delta = factor * stat_v[h, t, 2:3] + jnp.sum(prob * dprob, 0, keepdims=True)
            dscore = (prob * (dprob - delta)).astype(jnp.bfloat16)
            dfront_v[h, t] = dscore
            stat_v[h, t, 3:4] = factor
            stat_v[h, t, 4:5] = delta
            front_value += dot(prob.astype(jnp.bfloat16), grad, NN)
            front_key += dot(dscore, query, NN)
        front_key = front_key * SCALE
        for q in range(n_p):
            part_send[i, q] = jnp.concatenate(
                [front_key[q * own:(q + 1) * own], front_value[q * own:(q + 1) * own]], 0
            ).astype(jnp.bfloat16)

        @pl.when(me_r != h * stride)
        def _():
            part_copy(i, 0).start()

        @pl.when(me_r == h * stride)
        def _():
            part_recv[me] = part_send[i, me_p]

        for step in range(1, n_p):
            part_copy(i, step).start()

    def total_copy(i, step):
        return pltpu.make_async_remote_copy(
            src_ref=total_v.at[i], dst_ref=total_v.at[i],
            send_sem=total_ssem.at[step], recv_sem=total_rsem.at[i],
            device_id=(me_p, peers_r[step]), device_id_type=MESH)

    def add_up(i):
        @pl.when(me_r == order[i] * stride)
        def _():
            others = part_recv.at[pl.ds(0, n_dev - 1)]
            pltpu.make_async_copy(others, others, part_rsem).wait()

            def body(s, totals):
                prompt = group_ref[s]
                piece = part_recv[s].astype(jnp.float32)
                return tuple(
                    total + jnp.where(prompt == p, piece, 0.0) for p, total in enumerate(totals))

            zero = jnp.zeros(part_recv.shape[1:], jnp.float32)
            totals = lax.fori_loop(0, n_dev, body, (zero,) * prompts)
            for p in range(prompts):
                total_v[i, p] = totals[p].astype(jnp.bfloat16)
            for step in range(1, n_r):
                total_copy(i, step).start()

    stores = []

    def store(ref, out):
        copy = pltpu.make_async_copy(ref, out, store_sem.at[len(stores)])
        copy.start()
        stores.append(copy)

    def resp_terms(i):
        h = order[i]
        lanes = lanes_of(h)
        key_sums, value_sums = [], []
        for t in range(tiles):
            depth = (t + 1) * TILE
            query = stacked(query_v, h, t)
            prob = weight_v[h, t, 0:depth] * stat_v[h, t, 3:4]
            dscore = (prob * (dprob_v[h, t, 0:depth] - stat_v[h, t, 4:5])).astype(jnp.bfloat16)
            value_sums.append(dot(prob.astype(jnp.bfloat16), live_grad_v[h, t], NN))
            key_sums.append(dot(dscore, query, NN))
            turned = dot(
                keys_v[0:front + depth, lanes],
                jnp.concatenate([dfront_v[h, t], dscore], 0), TN) * SCALE
            turned = turned.astype(jnp.bfloat16)
            for g in range(GROUP):
                dquery_v[t * TILE:(t + 1) * TILE, (h * GROUP + g) * HD:(h * GROUP + g + 1) * HD] = (
                    turned[:, g * TILE:(g + 1) * TILE].T)
        for t in range(tiles):
            span = slice(t * TILE, (t + 1) * TILE)
            dkey_v[span, lanes] = (
                sum(s[span] for s in key_sums[t:]) * SCALE).astype(jnp.bfloat16)
            dvalue_v[span, lanes] = sum(s[span] for s in value_sums[t:]).astype(jnp.bfloat16)
        cols = pl.ds(h * wide, wide)
        store(dquery_v.at[:, cols], dquery_hbm.at[0, :, cols])

    loads["k"].wait()
    loads["v"].wait()
    resp_scores(0)

    loads["pk"].wait()
    loads["pv"].wait()

    def front_of(q):
        prompt = group_ref[q * n_r + me_r]
        return jnp.concatenate(
            [pkeys_v[prompt].astype(jnp.float32), pvalues_v[prompt].astype(jnp.float32)], 0
        ).astype(jnp.bfloat16)

    for q in range(n_p):
        front_send[q] = front_of(q)
    front_recv[me_p] = front_of(me_p)
    pl.semaphore_wait(barrier, n_dev - 1)

    front_copies = []
    for step in range(1, n_p):
        to = peers_p[step]
        copy = pltpu.make_async_remote_copy(
            src_ref=front_send.at[to], dst_ref=front_recv.at[me_p],
            send_sem=front_ssem.at[step], recv_sem=front_rsem.at[me_p],
            device_id=(to, me_r), device_id_type=MESH)
        copy.start()
        front_copies.append(copy)

    for i in range(1, KVH):
        resp_scores(i)

    for step in range(1, n_p):
        source = peers_p[step]
        pltpu.make_async_remote_copy(
            src_ref=front_send.at[source], dst_ref=front_recv.at[source],
            send_sem=front_ssem.at[step], recv_sem=front_rsem.at[source],
            device_id=(source, me_r), device_id_type=MESH).wait_recv()
    arrived = [front_recv[q].astype(jnp.float32) for q in range(n_p)]
    keys_v[0:front] = jnp.concatenate([a[0:own] for a in arrived], 0).astype(jnp.bfloat16)
    values_v[0:front] = jnp.concatenate([a[own:] for a in arrived], 0).astype(jnp.bfloat16)

    for i in range(KVH):
        front_terms(i)
    resp_terms(0)
    resp_terms(1)
    for i in range(KVH):
        add_up(i)
    resp_terms(2)
    resp_terms(3)
    store(dkey_v, dkey_hbm.at[0])
    store(dvalue_v, dvalue_hbm.at[0])

    for i, h in enumerate(order):
        @pl.when(me_r != h * stride)
        def _():
            total_copy(i, 1).wait_recv()

        total_ref[h] = total_v[i]

    for copy in stores:
        copy.wait()
    for copy in front_copies:
        copy.wait_send()
    for i, h in enumerate(order):
        @pl.when(me_r != h * stride)
        def _():
            part_copy(i, 0).wait_send()

        for step in range(1, n_p):
            part_copy(i, step).wait_send()

        @pl.when(me_r == h * stride)
        def _():
            for step in range(1, n_r):
                total_copy(i, step).wait_send()


def write_out(
    dquery, dkey, dvalue, total, dquery_out, dkey_out, dvalue_out, dpkey, dpvalue,
    dquery_v, dkey_v, dvalue_v, in_sem, out_sem,
):
    moves = []
    cut = dquery.shape[1] // PIECES
    spans = [(dkey, dkey_v, dkey_out, pl.ds(0, dkey.shape[1]))]
    spans.append((dvalue, dvalue_v, dvalue_out, pl.ds(0, dvalue.shape[1])))
    for n in range(PIECES):
        spans.append((dquery, dquery_v, dquery_out, pl.ds(n * cut, cut)))
    for n, (src, mid, dst, rows) in enumerate(spans):
        come = pltpu.make_async_copy(src.at[0, rows], mid.at[rows], in_sem.at[n])
        go = pltpu.make_async_copy(mid.at[rows], dst.at[0, rows], out_sem.at[n])
        come.start()
        moves.append((come, go))
    for come, go in moves:
        come.wait()
        go.start()
    own = dpkey.shape[1]
    for h in range(KVH):
        both = total[h].astype(jnp.float32)
        dpkey[:, :, h * HD:(h + 1) * HD] = both[:, 0:own]
        dpvalue[:, :, h * HD:(h + 1) * HD] = both[:, own:]
    for come, go in moves:
        go.wait()


def shards(n_p, n_r, query, resp_keys, resp_values, prompt_keys, prompt_values, out_grad, group, lengths):
    rows = query.shape[1]
    prompts, own, kvw = prompt_keys.shape
    front = own * n_p
    n_dev = n_p * n_r
    tiles = rows // TILE
    order = (0, 3, 1, 2)
    low = jnp.bfloat16
    vmem = pl.BlockSpec(memory_space=pltpu.VMEM)
    smem = pl.BlockSpec(memory_space=pltpu.SMEM)
    some = pl.BlockSpec(memory_space=pl.ANY)
    hbm = pl.BlockSpec(memory_space=pltpu.HBM)
    dma = pltpu.SemaphoreType.DMA
    like = lambda x, dtype: jax.ShapeDtypeStruct(x.shape, dtype)
    dquery, dkey, dvalue, total = pl.pallas_call(
        functools.partial(kernel, n_p, n_r, order),
        out_shape=(
            like(query, low), like(resp_keys, low), like(resp_values, low),
            jax.ShapeDtypeStruct((KVH, prompts, 2 * own, HD), low),
        ),
        in_specs=[smem, smem] + [hbm] * 6,
        out_specs=(some, some, some, vmem),
        scratch_shapes=[
            pltpu.VMEM((rows, QH * HD), low),
            pltpu.VMEM((rows, QH * HD), low),
            pltpu.VMEM((KVH, tiles, GROUP * TILE, HD), low),
            pltpu.VMEM((front + rows, kvw), low),
            pltpu.VMEM((front + rows, kvw), low),
            pltpu.VMEM((prompts, own, kvw), low),
            pltpu.VMEM((prompts, own, kvw), low),
            pltpu.VMEM((TILE, TILE), jnp.float32),
            pltpu.VMEM((KVH, tiles, rows, GROUP * TILE), jnp.float32),
            pltpu.VMEM((KVH, tiles, rows, GROUP * TILE), jnp.float32),
            pltpu.VMEM((KVH, tiles, 8, GROUP * TILE), jnp.float32),
            pltpu.VMEM((KVH, tiles, front, GROUP * TILE), low),
            pltpu.VMEM((rows, QH * HD), low),
            pltpu.VMEM((rows, kvw), low),
            pltpu.VMEM((rows, kvw), low),
            pltpu.VMEM((n_p, 2 * own, kvw), low),
            pltpu.VMEM((n_p, 2 * own, kvw), low),
            pltpu.VMEM((KVH, n_p, 2 * own, HD), low),
            pltpu.VMEM((n_dev, 2 * own, HD), low),
            pltpu.VMEM((KVH, prompts, 2 * own, HD), low),
            dma((5 + 2 * KVH,)),
            dma((2 + KVH,)),
            dma((n_p,)),
            dma((n_p,)),
            dma((KVH, n_p)),
            dma,
            dma((n_r,)),
            dma((KVH,)),
        ],
        compiler_params=pltpu.CompilerParams(
            collective_id=0, has_side_effects=True, vmem_limit_bytes=60 * 1024 * 1024),
    )(group, lengths, query, out_grad, resp_keys, resp_values, prompt_keys, prompt_values)
    return pl.pallas_call(
        write_out,
        out_shape=(
            like(query, low), like(resp_keys, low), like(resp_values, low),
            like(prompt_keys, jnp.float32), like(prompt_values, jnp.float32),
        ),
        in_specs=[some, some, some, vmem],
        out_specs=(some, some, some, vmem, vmem),
        scratch_shapes=[
            pltpu.VMEM((rows, QH * HD), low),
            pltpu.VMEM((rows, kvw), low),
            pltpu.VMEM((rows, kvw), low),
            dma((2 + PIECES,)),
            dma((2 + PIECES,)),
        ],
        compiler_params=pltpu.CompilerParams(vmem_limit_bytes=60 * 1024 * 1024),
    )(dquery, dkey, dvalue, total)


def solution(mesh):
    return jax.shard_map(
        functools.partial(shards, mesh.shape["prompt"], mesh.shape["resp"]),
        mesh=mesh,
        in_specs=(
            P(("prompt", "resp"), None, None),
            P(("prompt", "resp"), None, None),
            P(("prompt", "resp"), None, None),
            P(None, "prompt", None),
            P(None, "prompt", None),
            P(("prompt", "resp"), None, None),
            P(),
            P(("prompt", "resp")),
        ),
        out_specs=(
            P(("prompt", "resp"), None, None),
            P(("prompt", "resp"), None, None),
            P(("prompt", "resp"), None, None),
            P(None, "prompt", None),
            P(None, "prompt", None),
        ),
        check_vma=False,
    )
```

profile of v0, /device:TPU:0, one launch (start us, length us, event | category | flops | bytes accessed | tf_op | source)
XLA Modules:
  0.0 28.6 jit_solution(9791619544496122454)
XLA Ops:
  1.3 23.5 %shard_map.119 = (bf16[1,256,2048]{2,1,0:T(8,128)(2,1)}, bf16[1,256,512]{2,1,0:T(8,128)(2,1)}, bf16[1,256,512]{2,1,0:T(8,128)(2,1)}, bf16[4,8,16,128]{3,2,1,0:T(8,128)(2,1)}) custom-call(s32[32]{0:T(128)} %group_ref.1, s32[1]{0:T(128)S(6)} %copy.13.length_ref, bf16[1,256,2048]{2,1,0:T(8,128)(2,1)} %query_hbm.1, bf16[1,256,2048]{2,1,0:T(8,128)(2,1)} %grad_hbm.1, ...), custom_call_target="tpu_custom_call" | custom-call | tf_op jit(solution)/shard_map/pallas_call | solution.py:342
  24.8 3.8 %shard_map.120 = (bf16[1,256,2048]{2,1,0:T(8,128)(2,1)}, bf16[1,256,512]{2,1,0:T(8,128)(2,1)}, bf16[1,256,512]{2,1,0:T(8,128)(2,1)}, f32[8,8,512]{2,1,0:T(8,128)}, f32[8,8,512]{2,1,0:T(8,128)}) custom-call(bf16[1,256,2048]{2,1,0:T(8,128)(2,1)} %get-tuple-element.9.dquery, bf16[1,256,512]{2,1,0:T(8,128)(2,1)} %get-tuple-element.10.dkey, ...), custom_call_target="tpu_custom_call" | custom-call | tf_op jit(solution)/shard_map/pallas_call | solution.py:383
where the time goes:
time: 28.8 us; the launch traced here: 28.6 us
  Pallas kernels  27.3 us (95%)
  between operations  1.29 us (4%)
    pallas_call x1, Pallas kernels, shards(): pl.pallas_call(functools.partial(kernel, n_p, n_r, order), out_shape=(lik...  23.5 us
    pallas_call x1, Pallas kernels, shards(): pl.pallas_call(write_out, out_shape=(like(query, low), like(resp_keys, lo...  3.79 us

commit v1 on v0

--- a/solution.py
+++ b/solution.py
@@ -265,9 +265,11 @@
     for i in range(KVH):
         front_terms(i)
     resp_terms(0)
+    add_up(0)
+    add_up(1)
     resp_terms(1)
-    for i in range(KVH):
-        add_up(i)
+    add_up(2)
+    add_up(3)
     resp_terms(2)
     resp_terms(3)
     store(dkey_v, dkey_hbm.at[0])
@@ -298,31 +300,22 @@
                 total_copy(i, step).wait_send()
 
 
-def write_out(
-    dquery, dkey, dvalue, total, dquery_out, dkey_out, dvalue_out, dpkey, dpvalue,
-    dquery_v, dkey_v, dvalue_v, in_sem, out_sem,
-):
-    moves = []
+def write_out(dquery, dkey, dvalue, total, dquery_out, dkey_out, dvalue_out, dpkey, dpvalue, sem):
+    copies = []
     cut = dquery.shape[1] // PIECES
-    spans = [(dkey, dkey_v, dkey_out, pl.ds(0, dkey.shape[1]))]
-    spans.append((dvalue, dvalue_v, dvalue_out, pl.ds(0, dvalue.shape[1])))
-    for n in range(PIECES):
-        spans.append((dquery, dquery_v, dquery_out, pl.ds(n * cut, cut)))
-    for n, (src, mid, dst, rows) in enumerate(spans):
-        come = pltpu.make_async_copy(src.at[0, rows], mid.at[rows], in_sem.at[n])
-        go = pltpu.make_async_copy(mid.at[rows], dst.at[0, rows], out_sem.at[n])
-        come.start()
-        moves.append((come, go))
-    for come, go in moves:
-        come.wait()
-        go.start()
+    spans = [(dquery, dquery_out, pl.ds(n * cut, cut)) for n in range(PIECES)]
+    spans.append((dkey, dkey_out, pl.ds(0, dkey.shape[1])))
+    spans.append((dvalue, dvalue_out, pl.ds(0, dvalue.shape[1])))
+    for n, (src, dst, rows) in enumerate(spans):
+        copies.append(pltpu.make_async_copy(src.at[0, rows], dst.at[0, rows], sem.at[n]))
+        copies[-1].start()
     own = dpkey.shape[1]
     for h in range(KVH):
         both = total[h].astype(jnp.float32)
         dpkey[:, :, h * HD:(h + 1) * HD] = both[:, 0:own]
         dpvalue[:, :, h * HD:(h + 1) * HD] = both[:, own:]
-    for come, go in moves:
-        go.wait()
+    for copy in copies:
+        copy.wait()
 
 
 def shards(n_p, n_r, query, resp_keys, resp_values, prompt_keys, prompt_values, out_grad, group, lengths):
@@ -342,8 +335,8 @@
     dquery, dkey, dvalue, total = pl.pallas_call(
         functools.partial(kernel, n_p, n_r, order),
         out_shape=(
-            like(query, low), like(resp_keys, low), like(resp_values, low),
-            jax.ShapeDtypeStruct((KVH, prompts, 2 * own, HD), low),
+            pltpu.VMEM(query.shape, low), pltpu.VMEM(resp_keys.shape, low),
+            pltpu.VMEM(resp_values.shape, low), pltpu.VMEM((KVH, prompts, 2 * own, HD), low),
         ),
         in_specs=[smem, smem] + [hbm] * 6,
         out_specs=(some, some, some, vmem),
@@ -388,14 +381,8 @@
         ),
         in_specs=[some, some, some, vmem],
         out_specs=(some, some, some, vmem, vmem),
-        scratch_shapes=[
-            pltpu.VMEM((rows, QH * HD), low),
-            pltpu.VMEM((rows, kvw), low),
-            pltpu.VMEM((rows, kvw), low),
-            dma((2 + PIECES,)),
-            dma((2 + PIECES,)),
-        ],
-        compiler_params=pltpu.CompilerParams(vmem_limit_bytes=60 * 1024 * 1024),
+        scratch_shapes=[dma((2 + PIECES,))],
+        compiler_params=pltpu.CompilerParams(vmem_limit_bytes=16 * 1024 * 1024),
     )(dquery, dkey, dvalue, total)
 
 

time: 28.8 us -> 26.2 us (0.910)
  Pallas kernels: 27.3 us -> 24.7 us
    pallas_call x1, Pallas kernels: 3.79 us -> 1.89 us  [shards(): pl.pallas_call(write_out, out_shape=(like(query, low), like(resp_keys, lo...]
    pallas_call x1, Pallas kernels: 23.5 us -> 22.8 us  [shards(): pl.pallas_call(functools.partial(kernel, n_p, n_r, order), out_shape=(plt...]
where the time goes in v1:
time: 26.2 us; the launch traced here: 26 us
  Pallas kernels  24.7 us (94%)
  between operations  1.29 us (5%)
    pallas_call x1, Pallas kernels, shards(): pl.pallas_call(functools.partial(kernel, n_p, n_r, order), out_shape=(plt...  22.8 us
    pallas_call x1, Pallas kernels, shards(): pl.pallas_call(write_out, out_shape=(like(query, low), like(resp_keys, lo...  1.89 us

profile of v1, /device:TPU:0, one launch (start us, length us, event | category | flops | bytes accessed | tf_op | source)
XLA Modules:
  0.0 26.0 jit_solution(14905358491316334144)
XLA Ops:
  1.3 22.8 %shard_map.119 = (bf16[1,256,2048]{2,1,0:T(8,128)(2,1)S(1)}, bf16[1,256,512]{2,1,0:T(8,128)(2,1)S(1)}, bf16[1,256,512]{2,1,0:T(8,128)(2,1)S(1)}, bf16[4,8,16,128]{3,2,1,0:T(8,128)(2,1)S(1)}) custom-call(s32[32]{0:T(128)} %group_ref.1, s32[1]{0:T(128)S(6)} %copy.13.length_ref, bf16[1,256,2048]{2,1,0:T(8,128)(2,1)} %query_hbm.1, ...), custom_call_target="tpu_custom_call" | custom-call | tf_op jit(solution)/shard_map/pallas_call | solution.py:335
  24.1 1.9 %shard_map.120 = (bf16[1,256,2048]{2,1,0:T(8,128)(2,1)}, bf16[1,256,512]{2,1,0:T(8,128)(2,1)}, bf16[1,256,512]{2,1,0:T(8,128)(2,1)}, f32[8,8,512]{2,1,0:T(8,128)}, f32[8,8,512]{2,1,0:T(8,128)}) custom-call(bf16[1,256,2048]{2,1,0:T(8,128)(2,1)S(1)} %get-tuple-element.9.dquery, bf16[1,256,512]{2,1,0:T(8,128)(2,1)S(1)} %get-tuple-element.10.dkey, ...), custom_call_target="tpu_custom_call" | custom-call | tf_op jit(solution)/shard_map/pallas_call | solution.py:376

commit v2 on v1

--- a/solution.py
+++ b/solution.py
@@ -249,8 +249,7 @@
         copy.start()
         front_copies.append(copy)
 
-    for i in range(1, KVH):
-        resp_scores(i)
+    resp_scores(1)
 
     for step in range(1, n_p):
         source = peers_p[step]
@@ -262,14 +261,18 @@
     keys_v[0:front] = jnp.concatenate([a[0:own] for a in arrived], 0).astype(jnp.bfloat16)
     values_v[0:front] = jnp.concatenate([a[own:] for a in arrived], 0).astype(jnp.bfloat16)
 
-    for i in range(KVH):
-        front_terms(i)
-    resp_terms(0)
+    front_terms(0)
+    front_terms(1)
+    resp_scores(2)
+    front_terms(2)
+    resp_scores(3)
+    front_terms(3)
     add_up(0)
     add_up(1)
-    resp_terms(1)
+    resp_terms(0)
     add_up(2)
     add_up(3)
+    resp_terms(1)
     resp_terms(2)
     resp_terms(3)
     store(dkey_v, dkey_hbm.at[0])

time: 26.2 us -> 26.2 us (level)
  no operation moved by 1% of the time
where the time goes in v2:
time: 26.2 us; the launch traced here: 26 us
  Pallas kernels  24.7 us (94%)
  between operations  1.29 us (5%)
    pallas_call x1, Pallas kernels, shards(): pl.pallas_call(functools.partial(kernel, n_p, n_r, order), out_shape=(plt...  22.8 us
    pallas_call x1, Pallas kernels, shards(): pl.pallas_call(write_out, out_shape=(like(query, low), like(resp_keys, lo...  1.89 us

profile of v2, /device:TPU:0, one launch (start us, length us, event | category | flops | bytes accessed | tf_op | source)
XLA Modules:
  0.0 26.0 jit_solution(5422886841697754715)
XLA Ops:
  1.3 22.8 %shard_map.119 = (bf16[1,256,2048]{2,1,0:T(8,128)(2,1)S(1)}, bf16[1,256,512]{2,1,0:T(8,128)(2,1)S(1)}, bf16[1,256,512]{2,1,0:T(8,128)(2,1)S(1)}, bf16[4,8,16,128]{3,2,1,0:T(8,128)(2,1)S(1)}) custom-call(s32[32]{0:T(128)} %group_ref.1, s32[1]{0:T(128)S(6)} %copy.13.length_ref, bf16[1,256,2048]{2,1,0:T(8,128)(2,1)} %query_hbm.1, ...), custom_call_target="tpu_custom_call" | custom-call | tf_op jit(solution)/shard_map/pallas_call | solution.py:338
  24.1 1.9 %shard_map.120 = (bf16[1,256,2048]{2,1,0:T(8,128)(2,1)}, bf16[1,256,512]{2,1,0:T(8,128)(2,1)}, bf16[1,256,512]{2,1,0:T(8,128)(2,1)}, f32[8,8,512]{2,1,0:T(8,128)}, f32[8,8,512]{2,1,0:T(8,128)}) custom-call(bf16[1,256,2048]{2,1,0:T(8,128)(2,1)S(1)} %get-tuple-element.9.dquery, bf16[1,256,512]{2,1,0:T(8,128)(2,1)S(1)} %get-tuple-element.10.dkey, ...), custom_call_target="tpu_custom_call" | custom-call | tf_op jit(solution)/shard_map/pallas_call | solution.py:379

commit v3 on v2

--- a/solution.py
+++ b/solution.py
@@ -14,6 +14,7 @@
 GROUP = QH // KVH
 TILE = 128
 PIECES = 4
+EARLY = 2
 MESH = pl.DeviceIdType.MESH
 MASKED = -1e30
 SCALE = 1.0 / math.sqrt(HD)
@@ -31,7 +32,7 @@
     group_ref, length_ref, query_hbm, grad_hbm, rkeys_hbm, rvalues_hbm, pkeys_hbm, pvalues_hbm,
     dquery_hbm, dkey_hbm, dvalue_hbm, total_ref,
     query_v, grad_v, live_grad_v, keys_v, values_v, pkeys_v, pvalues_v,
-    bias_v, weight_v, dprob_v, stat_v, dfront_v, dquery_v, dkey_v, dvalue_v,
+    bias_v, weight_v, dprob_v, stat_v, dfront_v, dscore_v, dquery_v, dkey_v, dvalue_v,
     front_send, front_recv, part_send, part_recv, total_v,
     load_sem, store_sem, front_ssem, front_rsem, part_ssem, part_rsem, total_ssem, total_rsem,
 ):
@@ -146,7 +147,10 @@
             stat_v[h, t, 4:5] = delta
             front_value += dot(prob.astype(jnp.bfloat16), grad, NN)
             front_key += dot(dscore, query, NN)
-        front_key = front_key * SCALE
+        send_part(i, front_key * SCALE, front_value)
+
+    def send_part(i, front_key, front_value):
+        h = order[i]
         for q in range(n_p):
             part_send[i, q] = jnp.concatenate(
                 [front_key[q * own:(q + 1) * own], front_value[q * own:(q + 1) * own]], 0
@@ -195,6 +199,12 @@
         copy.start()
         stores.append(copy)
 
+    def put_dquery(h, t, turned):
+        turned = (turned * SCALE).astype(jnp.bfloat16)
+        for g in range(GROUP):
+            dquery_v[t * TILE:(t + 1) * TILE, (h * GROUP + g) * HD:(h * GROUP + g + 1) * HD] = (
+                turned[:, g * TILE:(g + 1) * TILE].T)
+
     def resp_terms(i):
         h = order[i]
         lanes = lanes_of(h)
@@ -206,18 +216,56 @@
             dscore = (prob * (dprob_v[h, t, 0:depth] - stat_v[h, t, 4:5])).astype(jnp.bfloat16)
             value_sums.append(dot(prob.astype(jnp.bfloat16), live_grad_v[h, t], NN))
             key_sums.append(dot(dscore, query, NN))
-            turned = dot(
+            put_dquery(h, t, dot(
                 keys_v[0:front + depth, lanes],
-                jnp.concatenate([dfront_v[h, t], dscore], 0), TN) * SCALE
-            turned = turned.astype(jnp.bfloat16)
-            for g in range(GROUP):
-                dquery_v[t * TILE:(t + 1) * TILE, (h * GROUP + g) * HD:(h * GROUP + g + 1) * HD] = (
-                    turned[:, g * TILE:(g + 1) * TILE].T)
+                jnp.concatenate([dfront_v[h, t], dscore], 0), TN))
         for t in range(tiles):
             span = slice(t * TILE, (t + 1) * TILE)
             dkey_v[span, lanes] = (
                 sum(s[span] for s in key_sums[t:]) * SCALE).astype(jnp.bfloat16)
             dvalue_v[span, lanes] = sum(s[span] for s in value_sums[t:]).astype(jnp.bfloat16)
+        cols = pl.ds(h * wide, wide)
+        store(dquery_v.at[:, cols], dquery_hbm.at[0, :, cols])
+
+    def whole_scores(i):
+        h = order[i]
+        lanes = lanes_of(h)
+        loads["q", h].wait()
+        loads["g", h].wait()
+        key_sums, value_sums = [], []
+        for t in range(tiles):
+            depth = front + (t + 1) * TILE
+            query = stacked(query_v, h, t)
+            grad = stacked(grad_v, h, t) * jnp.concatenate(
+                [live[t * TILE:(t + 1) * TILE]] * GROUP, 0)
+            scores = dot(keys_v[0:depth, lanes], query, NT)
+            scores = jnp.concatenate(
+                [scores[:depth - TILE],
+                 scores[depth - TILE:] + jnp.concatenate([bias_v[...]] * GROUP, 1)], 0)
+            top = jnp.max(scores, 0, keepdims=True)
+            weights = jnp.exp2((scores - top) * power)
+            prob = weights * (1.0 / jnp.sum(weights, 0, keepdims=True))
+            dprob = dot(values_v[0:depth, lanes], grad, NT)
+            delta = jnp.sum(prob * dprob, 0, keepdims=True)
+            dscore = (prob * (dprob - delta)).astype(jnp.bfloat16)
+            dscore_v[i - EARLY, t, 0:depth] = dscore
+            value_sums.append(dot(prob.astype(jnp.bfloat16), grad, NN))
+            key_sums.append(dot(dscore, query, NN))
+        send_part(i, sum(s[:front] for s in key_sums) * SCALE, sum(s[:front] for s in value_sums))
+        for t in range(tiles):
+            span = slice(t * TILE, (t + 1) * TILE)
+            low = front + t * TILE
+            dkey_v[span, lanes] = (
+                sum(s[low:low + TILE] for s in key_sums[t:]) * SCALE).astype(jnp.bfloat16)
+            dvalue_v[span, lanes] = sum(
+                s[low:low + TILE] for s in value_sums[t:]).astype(jnp.bfloat16)
+
+    def whole_terms(i):
+        h = order[i]
+        for t in range(tiles):
+            depth = front + (t + 1) * TILE
+            put_dquery(h, t, dot(
+                keys_v[0:depth, lanes_of(h)], dscore_v[i - EARLY, t, 0:depth], TN))
         cols = pl.ds(h * wide, wide)
         store(dquery_v.at[:, cols], dquery_hbm.at[0, :, cols])
 
@@ -263,18 +311,16 @@
 
     front_terms(0)
     front_terms(1)
-    resp_scores(2)
-    front_terms(2)
-    resp_scores(3)
-    front_terms(3)
+    whole_scores(2)
+    whole_scores(3)
     add_up(0)
     add_up(1)
     resp_terms(0)
     add_up(2)
     add_up(3)
     resp_terms(1)
-    resp_terms(2)
-    resp_terms(3)
+    whole_terms(2)
+    whole_terms(3)
     store(dkey_v, dkey_hbm.at[0])
     store(dvalue_v, dvalue_hbm.at[0])
 
@@ -356,6 +402,7 @@
             pltpu.VMEM((KVH, tiles, rows, GROUP * TILE), jnp.float32),
             pltpu.VMEM((KVH, tiles, 8, GROUP * TILE), jnp.float32),
             pltpu.VMEM((KVH, tiles, front, GROUP * TILE), low),
+            pltpu.VMEM((KVH - EARLY, tiles, front + rows, GROUP * TILE), low),
             pltpu.VMEM((rows, QH * HD), low),
             pltpu.VMEM((rows, kvw), low),
             pltpu.VMEM((rows, kvw), low),

time: 26.2 us -> 26.2 us (level)
  no operation moved by 1% of the time
where the time goes in v3:
time: 26.2 us; the launch traced here: 26 us
  Pallas kernels  24.7 us (94%)
  between operations  1.29 us (5%)
    pallas_call x1, Pallas kernels, shards(): pl.pallas_call(functools.partial(kernel, n_p, n_r, order), out_shape=(plt...  22.9 us
    pallas_call x1, Pallas kernels, shards(): pl.pallas_call(write_out, out_shape=(like(query, low), like(resp_keys, lo...  1.89 us

profile of v3, /device:TPU:0, one launch (start us, length us, event | category | flops | bytes accessed | tf_op | source)
XLA Modules:
  0.0 26.0 jit_solution(4304532912747566009)
XLA Ops:
  1.3 22.9 %shard_map.119 = (bf16[1,256,2048]{2,1,0:T(8,128)(2,1)S(1)}, bf16[1,256,512]{2,1,0:T(8,128)(2,1)S(1)}, bf16[1,256,512]{2,1,0:T(8,128)(2,1)S(1)}, bf16[4,8,16,128]{3,2,1,0:T(8,128)(2,1)S(1)}) custom-call(s32[32]{0:T(128)} %group_ref.1, s32[1]{0:T(128)S(6)} %copy.13.length_ref, bf16[1,256,2048]{2,1,0:T(8,128)(2,1)} %query_hbm.1, ...), custom_call_target="tpu_custom_call" | custom-call | tf_op jit(solution)/shard_map/pallas_call | solution.py:384
  24.1 1.9 %shard_map.120 = (bf16[1,256,2048]{2,1,0:T(8,128)(2,1)}, bf16[1,256,512]{2,1,0:T(8,128)(2,1)}, bf16[1,256,512]{2,1,0:T(8,128)(2,1)}, f32[8,8,512]{2,1,0:T(8,128)}, f32[8,8,512]{2,1,0:T(8,128)}) custom-call(bf16[1,256,2048]{2,1,0:T(8,128)(2,1)S(1)} %get-tuple-element.9.dquery, bf16[1,256,512]{2,1,0:T(8,128)(2,1)S(1)} %get-tuple-element.10.dkey, ...), custom_call_target="tpu_custom_call" | custom-call | tf_op jit(solution)/shard_map/pallas_call | solution.py:426
